TPU v7x, 512 devices: a whole 4x8x8 slice. The times are simulated.
512 devices in a mesh: dp: 16 (over y, core), tensor: 32 (over z, x).
Axes of the slice: x: 4, y: 8, z: 8, core: 2. Of those that a mesh axis runs over, the one named last changes fastest.
Arguments:
- x_in: bfloat16 [128, 128, 8192], P('dp', None, 'tensor'), may hold values from -16 to 16
- z_in: bfloat16 [128, 128, 8192], P('dp', None, 'tensor'), may hold values from -6 to 6
- b_in: bfloat16 [128, 128, 1024], P('dp'), may hold values from -1.5 to 1.5
- c_in: bfloat16 [128, 128, 1024], P('dp'), may hold values from -1.5 to 1.5
- dt_raw: float32 [128, 128, 128], P('dp', 'tensor'), may hold values from -4.2 to 5
- a_log: float32 [128], P('tensor'), may hold values from -3.52 to -0.91
- d_skip: float32 [128], P('tensor'), may hold values from 0.1 to 1.9
- norm_gain: float32 [8192], P('tensor'), may hold values from 0.1 to 1.9
- states: bfloat16 [128, 128, 64, 256], P('dp', 'tensor'), may hold values from -2 to 2
- dest: int32 [128], replicated, may hold values from 0 to 15, as said below
- accepted: int32 [128], replicated, may hold values from 1 to 128, as said below
Outputs:
- mixed: bfloat16 [128, 128, 8192], P('dp', None, 'tensor')
- new_states: bfloat16 [128, 128, 64, 256], P('dp', 'tensor')
Inputs may be any that keep to these rules, and one draw needn't show every extreme that they name: `dest`: every group is the destination of exactly 8 tiles. One group sends at most 1 tile to one other group, and exactly 1 to some group. The offsets (destination minus source, modulo the number of groups) that a group uses form the same set for every group; where 8 allows, that set holds half the number of groups, then 1, then minus 1. `accepted`: tile 0 and some others accept all 128 rows.
All inputs are finite; a program needn't handle non-finite values.
Results may differ from a plain program's by a relative error of at most 0.011.
Values may be sent and summed in bfloat16 or wider, within the bound.
No kernel may reach another device: no remote copies, remote signals or barrier semaphores. Data moves between devices by JAX's collectives and lax.ppermute only.
A program may use at most 64 MiB of HBM per device.

v0:
```python
import jax
import jax.numpy as jnp
from jax import lax
from jax.sharding import PartitionSpec as P

GROUPS = 4
CHANNELS = 8192


def block_arithmetic(x_in, b_in, c_in, dt_raw, a_log, d_skip, prefix, accepted):
    tile_count, row_count, channels = x_in.shape
    head_count = dt_raw.shape[1]
    state_width = prefix.shape[-1]
    head_width = channels // head_count
    group_count = b_in.shape[2] // state_width
    tiles_per_group = head_count // group_count
    b_groups = b_in.reshape(tile_count, row_count, group_count, state_width)
    c_groups = c_in.reshape(tile_count, row_count, group_count, state_width)
    step_size = jax.nn.softplus(dt_raw)
    cumulative = jnp.cumsum(-jnp.exp(a_log)[None, :, None] * step_size, axis=2)
    row_ids = lax.broadcasted_iota(jnp.int32, (row_count, row_count), 0)
    col_ids = lax.broadcasted_iota(jnp.int32, (row_count, row_count), 1)
    lower = col_ids <= row_ids
    spread = cumulative[:, :, :, None] - cumulative[:, :, None, :]
    decay = jnp.where(lower, jnp.exp(jnp.where(lower, spread, 0.0)), 0.0)
    products = jnp.einsum("slgn,smgn->sglm", c_groups, b_groups, preferred_element_type=jnp.float32)
    shaped = (tile_count, group_count, tiles_per_group, row_count, row_count)
    weights = (
        products[:, :, None]
        * decay.reshape(shaped)
        * step_size.reshape(tile_count, group_count, tiles_per_group, 1, row_count)
    ).astype(jnp.bfloat16)
    x_groups = x_in.reshape(tile_count, row_count, group_count, tiles_per_group, head_width)
    within = jnp.einsum("sghlm,smghp->slghp", weights, x_groups, preferred_element_type=jnp.float32)
    prefix_groups = prefix.reshape(
        tile_count, group_count, tiles_per_group, head_width, state_width
    )
    carried = jnp.einsum(
        "slgn,sghpn->slghp", c_groups, prefix_groups, preferred_element_type=jnp.float32
    )
    fading = (
        jnp.exp(cumulative)
        .reshape(tile_count, group_count, tiles_per_group, row_count)
        .transpose(0, 3, 1, 2)[..., None]
    )
    skip = d_skip.reshape(group_count, tiles_per_group)[None, None, :, :, None] * x_groups.astype(
        jnp.float32
    )
    ssm_out = (
        (within + fading * carried + skip)
        .reshape(tile_count, row_count, channels)
        .astype(jnp.bfloat16)
    )
    positions = lax.broadcasted_iota(jnp.int32, (tile_count, row_count), 1)
    last_row = positions == accepted[:, None] - 1
    kept = positions < accepted[:, None]
    final = jnp.sum(jnp.where(last_row[:, None, :], cumulative, 0.0), axis=2)
    gap = jnp.where(kept[:, None, :], final[:, :, None] - cumulative, 0.0)
    scale = jnp.where(kept[:, None, :], jnp.exp(gap), 0.0) * step_size
    scale_rows = scale.reshape(tile_count, group_count, tiles_per_group, row_count).transpose(
        0, 3, 1, 2
    )[..., None]
    inputs_kept = (x_groups.astype(jnp.float32) * scale_rows).astype(jnp.bfloat16)
    added = jnp.einsum(
        "slghp,slgn->sghpn", inputs_kept, b_groups, preferred_element_type=jnp.float32
    )
    fade_end = jnp.exp(final).reshape(tile_count, group_count, tiles_per_group)[..., None, None]
    new_state = fade_end * prefix_groups.astype(jnp.float32) + added
    return (ssm_out, new_state.reshape(prefix.shape).astype(jnp.bfloat16))


def routing(dest, own_group, group_count, tiles_dev, capacity):
    dest_table = dest.reshape(group_count, tiles_dev)
    tile_index = jnp.arange(tiles_dev, dtype=jnp.int32)
    same_dest = dest_table[:, :, None] == dest_table[:, None, :]
    before = tile_index[None, :] < tile_index[:, None]
    order_rank = jnp.sum(same_dest & before[None], axis=2)
    slot_place = dest_table * capacity + order_rank
    own_slots = jnp.take(slot_place, own_group, axis=0)
    slot_ids = jnp.arange(group_count * capacity, dtype=jnp.int32)
    sender = jnp.sum(
        jnp.where(own_slots[None, :] == slot_ids[:, None], tile_index[None, :], 0), axis=1
    )
    slot_turn = jnp.arange(capacity, dtype=jnp.int32)
    matched = (dest_table[:, None, :] == own_group) & (
        order_rank[:, None, :] == slot_turn[None, :, None]
    )
    is_live = jnp.any(matched, axis=2).reshape(-1)
    local_tile = jnp.sum(jnp.where(matched, tile_index[None, None, :], 0), axis=2)
    source_tile = (
        jnp.arange(group_count, dtype=jnp.int32)[:, None] * tiles_dev + local_tile
    ).reshape(-1)
    counted = is_live.astype(jnp.int32)
    compact_slot = jnp.cumsum(counted) - counted
    inverse = jnp.sum(
        jnp.where(
            is_live[None, :] & (compact_slot[None, :] == tile_index[:, None]), slot_ids[None, :], 0
        ),
        axis=1,
    )
    compact_slot = jnp.where(is_live, compact_slot, 0)
    return (own_slots, sender, source_tile, inverse, compact_slot)


def on_device(x_in, z_in, b_in, c_in, dt_raw, a_log, d_skip, norm_gain, states, dest, accepted):
    group_count = lax.axis_size("dp")
    tiles_dev = x_in.shape[0]
    capacity = (tiles_dev + group_count - 1) // group_count
    own_group = lax.axis_index("dp")
    state_width = states.shape[-1]
    head_group = lax.axis_index("tensor") // (lax.axis_size("tensor") // GROUPS)
    b_mine = lax.dynamic_slice_in_dim(b_in, head_group * state_width, state_width, 2)
    c_mine = lax.dynamic_slice_in_dim(c_in, head_group * state_width, state_width, 2)
    own_slots, sender, source_tile, inverse, compact_slot = routing(
        dest, own_group, group_count, tiles_dev, capacity
    )
    x_send = jnp.take(x_in, sender, axis=0)
    b_send = jnp.take(b_mine, sender, axis=0)
    c_send = jnp.take(c_mine, sender, axis=0)
    dt_send = jnp.take(dt_raw, sender, axis=0)
    x_got, b_got, c_got, dt_got = (
        lax.all_to_all(x_send, "dp", split_axis=0, concat_axis=0, tiled=True),
        lax.all_to_all(b_send, "dp", split_axis=0, concat_axis=0, tiled=True),
        lax.all_to_all(c_send, "dp", split_axis=0, concat_axis=0, tiled=True),
        lax.all_to_all(
            dt_send.astype(jnp.bfloat16), "dp", split_axis=0, concat_axis=0, tiled=True
        ).astype(dt_send.dtype),
    )
    accept_here = jnp.take(accepted, jnp.take(source_tile, inverse, axis=0), axis=0)
    ssm_here, new_states = block_arithmetic(
        jnp.take(x_got, inverse, axis=0),
        jnp.take(b_got, inverse, axis=0),
        jnp.take(c_got, inverse, axis=0),
        jnp.take(dt_got, inverse, axis=0),
        a_log,
        d_skip,
        states,
        accept_here,
    )
    returned = lax.all_to_all(
        jnp.take(ssm_here, compact_slot, axis=0), "dp", split_axis=0, concat_axis=0, tiled=True
    )
    ssm_out = jnp.take(returned, own_slots, axis=0)
    gated = ssm_out.astype(jnp.float32) * jax.nn.silu(z_in.astype(jnp.float32))
    local_squares = jnp.sum(gated * gated, axis=-1)
    group_pick = (jnp.arange(GROUPS, dtype=jnp.int32) == head_group).astype(jnp.float32)
    placed = local_squares[:, :, None] * group_pick
    square_total = lax.psum(placed, "tensor")
    group_total = jnp.sum(square_total * group_pick, axis=-1)
    factor = lax.rsqrt(group_total / (CHANNELS // GROUPS) + 1e-05)
    mixed = (gated * factor[:, :, None] * norm_gain).astype(jnp.bfloat16)
    return (mixed, new_states)


def solution(mesh):
    in_specs = (
        P("dp", None, "tensor"),
        P("dp", None, "tensor"),
        P("dp", None, None),
        P("dp", None, None),
        P("dp", "tensor", None),
        P("tensor"),
        P("tensor"),
        P("tensor"),
        P("dp", "tensor", None, None),
        P(),
        P(),
    )
    out_specs = (P("dp", None, "tensor"), P("dp", "tensor", None, None))
    return jax.shard_map(
        on_device, mesh=mesh, in_specs=in_specs, out_specs=out_specs, check_vma=False
    )
```

profile of v0, /device:TPU:24, one launch (start us, length us, event | category | flops | bytes accessed | tf_op | source)
XLA Modules:
  0.0 306.1 jit_solution(15042486600253870892)
XLA Ops:
  0.7 0.8 reshape.409
  2.0 1.3 gather_fusion
  3.3 0.7 select_convert_fusion
  4.0 8.9 %all-to-all-start.3 = ((bf16[16,4,128]{2,1,0:T(4,128)(2,1)}), bf16[16,4,128]{2,1,0:T(4,128)(2,1)S(1)}, u32[]{:S(2)}, u32[]{:S(2)}) async-start(bf16[16,4,128]{2,1,0:T(4,128)(2,1)} %select_convert_fusion), calls=%async_computation.3 | async-start | bytes 32768 | tf_op jit(solution)/shard_map/all_to_all | solution.py:125
  12.9 1.3 constant_dynamic-slice_fusion
  14.2 0.6 gather_fusion.6
  14.8 1.6 gather_fusion.8
  16.4 1.6 gather_fusion.4
  18.1 3.1 %broadcast_select_fusion.1 = (bf16[16,128,256]{2,1,0:T(8,128)(2,1)}, bf16[16,128,256]{2,1,0:T(8,128)(2,1)}, bf16[16,128,256]{2,1,0:T(8,128)(2,1)}) fusion(bf16[16,128,256]{2,1,0:T(8,128)(2,1)S(1)} %copy-done.2, pred[16]{0:T(512)(128)(4,1)S(1)} %compare_and_fusion.3, bf16[16,128,256]{2,1,0:T(8,128)(2,1)S(1)} %gather_fusion.6, ...), kind=kLoop, calls=%fused_computation.35 | loop fusion | flops 1572864 | bytes 6291472 | tf_op jit(solution)/shard_map/jit(_take)/select_n | solution.py:118
  21.2 33.6 %all_to_all.25 = bf16[16,128,256]{2,1,0:T(8,128)(2,1)S(1)} all-to-all(bf16[16,128,256]{2,1,0:T(8,128)(2,1)} %get-tuple-element.26), channel_id=1, replica_groups=mesh['dp'=16,'tensor'=32] {'dp'}, dimensions={0} | all-to-all | bytes 2097152 | tf_op jit(solution)/shard_map/all_to_all | solution.py:122
  54.8 5.2 %all-to-all-start.2 = ((bf16[16,128,256]{2,1,0:T(8,128)(2,1)}), bf16[16,128,256]{2,1,0:T(8,128)(2,1)S(1)}, u32[]{:S(2)}, u32[]{:S(2)}) async-start(bf16[16,128,256]{2,1,0:T(8,128)(2,1)} %get-tuple-element.24), calls=%async_computation.2 | async-start | bytes 2097152 | tf_op jit(solution)/shard_map/all_to_all | solution.py:123
  60.9 0.6 gather_fusion.2
  61.6 0.6 gather_fusion.3
  62.2 24.0 %all-to-all-done.2 = bf16[16,128,256]{2,1,0:T(8,128)(2,1)S(1)} async-done(((bf16[16,128,256]{2,1,0:T(8,128)(2,1)}), bf16[16,128,256]{2,1,0:T(8,128)(2,1)S(1)}, u32[]{:S(2)}, u32[]{:S(2)}) %all-to-all-start.2) | async-done | bytes 1048608 | tf_op jit(solution)/shard_map/all_to_all | solution.py:123
  86.3 5.2 %all-to-all-start.1 = ((bf16[16,128,256]{2,1,0:T(8,128)(2,1)}), bf16[16,128,256]{2,1,0:T(8,128)(2,1)}, u32[]{:S(2)}, u32[]{:S(2)}) async-start(bf16[16,128,256]{2,1,0:T(8,128)(2,1)} %get-tuple-element.25), calls=%async_computation.1 | async-start | bytes 2097152 | tf_op jit(solution)/shard_map/all_to_all | solution.py:124
  91.7 0.6 gather_fusion.1
  92.3 1.1 reduce_window_sum.20
  93.7 0.6 gather_fusion.5
  94.4 1.0 copy.85
  95.6 1.4 gather_fusion.9
  97.0 20.8 %all-to-all-done.1 = bf16[16,128,256]{2,1,0:T(8,128)(2,1)} async-done(((bf16[16,128,256]{2,1,0:T(8,128)(2,1)}), bf16[16,128,256]{2,1,0:T(8,128)(2,1)}, u32[]{:S(2)}, u32[]{:S(2)}) %all-to-all-start.1) | async-done | bytes 1048608 | tf_op jit(solution)/shard_map/all_to_all | solution.py:124
  117.8 1.8 gather_fusion.7
  119.7 1.5 fusion.17
  121.7 1.2 fusion.3
  123.1 0.6 gather_fusion.10
  123.7 1.2 broadcast_select_fusion
  124.9 5.2 %all-to-all-start.4 = ((bf16[16,128,256]{2,1,0:T(8,128)(2,1)}), bf16[16,128,256]{2,1,0:T(8,128)(2,1)S(1)}, u32[]{:S(2)}, u32[]{:S(2)}) async-start(bf16[16,128,256]{2,1,0:T(8,128)(2,1)} %broadcast_select_fusion), calls=%async_computation.4 | async-start | bytes 2097152 | tf_op jit(solution)/shard_map/all_to_all | solution.py:140
  130.2 2.7 add_convert_fusion
  133.0 23.3 %all-to-all-done.4 = bf16[16,128,256]{2,1,0:T(8,128)(2,1)S(1)} async-done(((bf16[16,128,256]{2,1,0:T(8,128)(2,1)}), bf16[16,128,256]{2,1,0:T(8,128)(2,1)S(1)}, u32[]{:S(2)}, u32[]{:S(2)}) %all-to-all-start.4) | async-done | bytes 1048608 | tf_op jit(solution)/shard_map/all_to_all | solution.py:140
  156.3 0.6 gather_fusion.11
  157.5 147.3 %psum.7 = f32[8,128,4]{1,0,2:T(8,128)S(1)} all-reduce(f32[8,128,4]{1,0,2:T(8,128)S(1)} %broadcast_multiply_fusion), channel_id=1, replica_groups=mesh['dp'=16,'tensor'=32] {'tensor'}, use_global_device_ids=true, to_apply=%region_7.10 | all-reduce | flops 4096 | bytes 32768 | tf_op jit(solution)/shard_map/psum | solution.py:148
  304.9 1.2 multiply_convert_fusion.3
  (80 shorter events, 3.6 us)
Async XLA Ops:
  0.6 15.8 %copy-start = (bf16[8,128,256]{2,1,0:T(8,128)(2,1)S(1)}, bf16[8,128,256]{2,1,0:T(8,128)(2,1)}, u32[]{:S(2)}) copy-start(bf16[8,128,256]{2,1,0:T(8,128)(2,1)} %param.15) | copy-start | bytes 1572868
  4.0 17.2 %all-to-all-start.3 = ((bf16[16,4,128]{2,1,0:T(4,128)(2,1)}), bf16[16,4,128]{2,1,0:T(4,128)(2,1)S(1)}, u32[]{:S(2)}, u32[]{:S(2)}) async-start(bf16[16,4,128]{2,1,0:T(4,128)(2,1)} %select_convert_fusion), calls=%async_computation.3 | async-start | bytes 32768 | tf_op jit(solution)/shard_map/all_to_all | solution.py:125
  16.4 1.7 copy-start.2
  21.2 38.8 %copy-start.8 = (s32[128]{0:T(128)S(1)}, s32[128]{0:T(128)}, u32[]{:S(2)}) copy-start(s32[128]{0:T(128)} %param.24) | copy-start | bytes 1540
  21.2 40.4 %copy-start.1 = (s32[128]{0:T(128)S(1)}, s32[128]{0:T(128)}, u32[]{:S(2)}) copy-start(s32[128]{0:T(128)} %param.25) | copy-start | bytes 1540
  54.8 31.5 %all-to-all-start.2 = ((bf16[16,128,256]{2,1,0:T(8,128)(2,1)}), bf16[16,128,256]{2,1,0:T(8,128)(2,1)S(1)}, u32[]{:S(2)}, u32[]{:S(2)}) async-start(bf16[16,128,256]{2,1,0:T(8,128)(2,1)} %get-tuple-element.24), calls=%async_computation.2 | async-start | bytes 2097152 | tf_op jit(solution)/shard_map/all_to_all | solution.py:123
  60.0 31.5 %copy-start.9 = (f32[4]{0:T(128)S(1)}, f32[4]{0:T(128)}, u32[]{:S(2)}) copy-start(f32[4]{0:T(128)} %param.20) | copy-start | bytes 52
  86.3 31.6 %all-to-all-start.1 = ((bf16[16,128,256]{2,1,0:T(8,128)(2,1)}), bf16[16,128,256]{2,1,0:T(8,128)(2,1)}, u32[]{:S(2)}, u32[]{:S(2)}) async-start(bf16[16,128,256]{2,1,0:T(8,128)(2,1)} %get-tuple-element.25), calls=%async_computation.1 | async-start | bytes 2097152 | tf_op jit(solution)/shard_map/all_to_all | solution.py:124
  97.0 24.1 %copy-start.4 = (bf16[8,4,64,256]{3,2,1,0:T(8,128)(2,1)S(1)}, bf16[8,4,64,256]{3,2,1,0:T(8,128)(2,1)}, u32[]{:S(2)}) copy-start(bf16[8,4,64,256]{3,2,1,0:T(8,128)(2,1)} %param.23) | copy-start | bytes 3145732
  119.6 2.0 copy-start.6
  119.6 2.0 copy-start.10
  123.7 6.5 %copy-start.5 = (bf16[8,4,64,256]{3,2,1,0:T(8,128)(2,1)S(1)}, bf16[8,4,64,256]{3,2,1,0:T(8,128)(2,1)}, u32[]{:S(2)}) copy-start(bf16[8,4,64,256]{3,2,1,0:T(8,128)(2,1)} %param.23) | copy-start | bytes 3145732
  124.9 31.5 %all-to-all-start.4 = ((bf16[16,128,256]{2,1,0:T(8,128)(2,1)}), bf16[16,128,256]{2,1,0:T(8,128)(2,1)S(1)}, u32[]{:S(2)}, u32[]{:S(2)}) async-start(bf16[16,128,256]{2,1,0:T(8,128)(2,1)} %broadcast_select_fusion), calls=%async_computation.4 | async-start | bytes 2097152 | tf_op jit(solution)/shard_map/all_to_all | solution.py:140
  130.2 26.7 %copy-start.3 = (bf16[8,128,256]{2,1,0:T(8,128)(2,1)S(1)}, bf16[8,128,256]{2,1,0:T(8,128)(2,1)}, u32[]{:S(2)}) copy-start(bf16[8,128,256]{2,1,0:T(8,128)(2,1)} %param.16) | copy-start | bytes 1572868
  130.2 174.6 %copy-start.7 = (f32[256]{0:T(256)S(1)}, f32[256]{0:T(256)}, u32[]{:S(2)}) copy-start(f32[256]{0:T(256)} %param.22) | copy-start | bytes 3076
where the time goes:
time: 307 us; the launch traced here: 306 us
  blocking collectives  181 us (59%)
  waiting for transfers between devices  68.2 us (22%)
  starting transfers between devices  24.6 us (8%)
  local copies, waits for them, and re-layouts  16 us (5%)
  other arithmetic  9.51 us (3%)
  matrix products  5.9 us (2%)
    psum x1, blocking collectives, on_device(): square_total = lax.psum(placed, 'tensor')  147 us
    all_to_all x1, blocking collectives, on_device(): lax.all_to_all(x_send, 'dp', split_axis=0, concat_axis=0, tiled=True)  33.6 us
    all_to_all x1, waiting for transfers between devices, on_device(): lax.all_to_all(b_send, 'dp', split_axis=0, concat_axis=0, tiled=True)  24 us
    all_to_all x1, waiting for transfers between devices, on_device(): lax.all_to_all(jnp.take(ssm_here, compact_slot, axis=0), 'dp', split_axis...  23.3 us
    all_to_all x1, waiting for transfers between devices, on_device(): lax.all_to_all(c_send, 'dp', split_axis=0, concat_axis=0, tiled=True)  20.8 us
    all_to_all x1, starting transfers between devices, on_device(): lax.all_to_all(dt_send.astype(jnp.bfloat16), 'dp', split_axis=0, concat_a...  8.91 us
  transfers between devices with their start and end apart: 4, of which 3 were waited for; matrix products, arithmetic and copies ran while one was open for 6% of the time, Pallas kernels for 0%

commit v1 on v0

--- a/solution.py
+++ b/solution.py
@@ -143,10 +143,14 @@
     ssm_out = jnp.take(returned, own_slots, axis=0)
     gated = ssm_out.astype(jnp.float32) * jax.nn.silu(z_in.astype(jnp.float32))
     local_squares = jnp.sum(gated * gated, axis=-1)
-    group_pick = (jnp.arange(GROUPS, dtype=jnp.int32) == head_group).astype(jnp.float32)
-    placed = local_squares[:, :, None] * group_pick
-    square_total = lax.psum(placed, "tensor")
-    group_total = jnp.sum(square_total * group_pick, axis=-1)
+    tensor_count = lax.axis_size("tensor")
+    group_size = tensor_count // GROUPS
+    group_members = [list(range(g * group_size, (g + 1) * group_size)) for g in range(GROUPS)]
+    copies = jnp.broadcast_to(local_squares[None], (group_size,) + local_squares.shape)
+    gathered = lax.all_to_all(
+        copies, "tensor", split_axis=0, concat_axis=0, axis_index_groups=group_members, tiled=True
+    )
+    group_total = jnp.sum(gathered, axis=0)
     factor = lax.rsqrt(group_total / (CHANNELS // GROUPS) + 1e-05)
     mixed = (gated * factor[:, :, None] * norm_gain).astype(jnp.bfloat16)
     return (mixed, new_states)

time: 307 us -> 172 us (0.56)
  the two profiles are of different devices: /device:TPU:24 before, /device:TPU:1 now
where the time goes in v1:
time: 172 us
  waiting for transfers between devices  76.8 us (45%)
  blocking collectives  36 us (21%)
  starting transfers between devices  25.9 us (15%)
  local copies, waits for them, and re-layouts  16.6 us (10%)
  other arithmetic  9.35 us (5%)
  matrix products  6.04 us (4%)
    all_to_all x1, blocking collectives, on_device(): lax.all_to_all(x_send, 'dp', split_axis=0, concat_axis=0, tiled=True)  36 us
    all_to_all x1, waiting for transfers between devices, on_device(): lax.all_to_all(jnp.take(ssm_here, compact_slot, axis=0), 'dp', split_axis...  27.8 us
    all_to_all x1, waiting for transfers between devices, on_device(): lax.all_to_all(b_send, 'dp', split_axis=0, concat_axis=0, tiled=True)  25.1 us
    all_to_all x1, waiting for transfers between devices, on_device(): lax.all_to_all(c_send, 'dp', split_axis=0, concat_axis=0, tiled=True)  21.8 us
    all_to_all x1, starting transfers between devices, on_device(): lax.all_to_all(dt_send.astype(jnp.bfloat16), 'dp', split_axis=0, concat_a...  10.2 us
    all_to_all x1, starting transfers between devices, on_device(): lax.all_to_all(copies, 'tensor', split_axis=0, concat_axis=0, axis_index_...  4.24 us
    all_to_all x1, starting transfers between devices, on_device(): lax.all_to_all(c_send, 'dp', split_axis=0, concat_axis=0, tiled=True)  4.23 us
    all_to_all x1, starting transfers between devices, on_device(): lax.all_to_all(jnp.take(ssm_here, compact_slot, axis=0), 'dp', split_axis...  3.68 us
  transfers between devices with their start and end apart: 5, of which 4 were waited for; matrix products, arithmetic and copies ran while one was open for 11% of the time, Pallas kernels for 0%

profile of v1, /device:TPU:1, one launch (start us, length us, event | category | flops | bytes accessed | tf_op | source)
XLA Modules:
  0.0 171.7 jit_solution(13432331773311912586)
XLA Ops:
  0.7 0.8 reshape.404
  2.0 1.3 gather_fusion
  3.3 0.7 select_convert_fusion
  4.0 10.2 %all-to-all-start.3 = ((bf16[16,4,128]{2,1,0:T(4,128)(2,1)}), bf16[16,4,128]{2,1,0:T(4,128)(2,1)S(1)}, u32[]{:S(2)}, u32[]{:S(2)}) async-start(bf16[16,4,128]{2,1,0:T(4,128)(2,1)} %select_convert_fusion), calls=%async_computation.3 | async-start | bytes 32768 | tf_op jit(solution)/shard_map/all_to_all | solution.py:125
  14.2 1.3 constant_dynamic-slice_fusion
  15.4 0.6 gather_fusion.6
  16.1 1.6 gather_fusion.8
  17.7 1.6 gather_fusion.4
  19.3 3.1 %broadcast_select_fusion.1 = (bf16[16,128,256]{2,1,0:T(8,128)(2,1)}, bf16[16,128,256]{2,1,0:T(8,128)(2,1)}, bf16[16,128,256]{2,1,0:T(8,128)(2,1)}) fusion(bf16[16,128,256]{2,1,0:T(8,128)(2,1)S(1)} %copy-done.2, pred[16]{0:T(512)(128)(4,1)S(1)} %compare_and_fusion.3, bf16[16,128,256]{2,1,0:T(8,128)(2,1)S(1)} %gather_fusion.6, ...), kind=kLoop, calls=%fused_computation.35 | loop fusion | flops 1572864 | bytes 6291472 | tf_op jit(solution)/shard_map/jit(_take)/select_n | solution.py:118
  22.4 36.0 %all_to_all.30 = bf16[16,128,256]{2,1,0:T(8,128)(2,1)S(1)} all-to-all(bf16[16,128,256]{2,1,0:T(8,128)(2,1)} %get-tuple-element.26), channel_id=1, replica_groups=mesh['dp'=16,'tensor'=32] {'dp'}, dimensions={0} | all-to-all | bytes 2097152 | tf_op jit(solution)/shard_map/all_to_all | solution.py:122
  58.4 3.6 %all-to-all-start.2 = ((bf16[16,128,256]{2,1,0:T(8,128)(2,1)}), bf16[16,128,256]{2,1,0:T(8,128)(2,1)S(1)}, u32[]{:S(2)}, u32[]{:S(2)}) async-start(bf16[16,128,256]{2,1,0:T(8,128)(2,1)} %get-tuple-element.24), calls=%async_computation.2 | async-start | bytes 2097152 | tf_op jit(solution)/shard_map/all_to_all | solution.py:123
  62.8 0.6 gather_fusion.2
  63.5 0.6 gather_fusion.3
  64.1 25.1 %all-to-all-done.2 = bf16[16,128,256]{2,1,0:T(8,128)(2,1)S(1)} async-done(((bf16[16,128,256]{2,1,0:T(8,128)(2,1)}), bf16[16,128,256]{2,1,0:T(8,128)(2,1)S(1)}, u32[]{:S(2)}, u32[]{:S(2)}) %all-to-all-start.2) | async-done | bytes 1048608 | tf_op jit(solution)/shard_map/all_to_all | solution.py:123
  89.2 4.2 %all-to-all-start.1 = ((bf16[16,128,256]{2,1,0:T(8,128)(2,1)}), bf16[16,128,256]{2,1,0:T(8,128)(2,1)}, u32[]{:S(2)}, u32[]{:S(2)}) async-start(bf16[16,128,256]{2,1,0:T(8,128)(2,1)} %get-tuple-element.25), calls=%async_computation.1 | async-start | bytes 2097152 | tf_op jit(solution)/shard_map/all_to_all | solution.py:124
  94.3 1.1 reduce_window_sum.20
  95.7 0.6 gather_fusion.5
  96.4 1.0 copy.85
  97.6 1.4 gather_fusion.9
  99.0 21.8 %all-to-all-done.1 = bf16[16,128,256]{2,1,0:T(8,128)(2,1)} async-done(((bf16[16,128,256]{2,1,0:T(8,128)(2,1)}), bf16[16,128,256]{2,1,0:T(8,128)(2,1)}, u32[]{:S(2)}, u32[]{:S(2)}) %all-to-all-start.1) | async-done | bytes 1048608 | tf_op jit(solution)/shard_map/all_to_all | solution.py:124
  120.8 1.8 %gather_fusion.7 = bf16[8,128,256]{2,1,0:T(8,128)(2,1)S(1)} fusion(bf16[16,128,256]{2,1,0:T(8,128)(2,1)} %all-to-all-done.1, s32[1024]{0:T(1024)S(1)} %pad_clamp_fusion.5), kind=kCustom, calls=%fused_computation.5.clone | custom fusion | bytes 1048608 | tf_op jit(solution)/shard_map/jit(_take)/gather | solution.py:133
  122.6 1.5 fusion.17
  124.7 1.2 fusion.3
  126.1 0.6 gather_fusion.10
  126.7 1.1 broadcast_select_fusion
  127.8 3.7 %all-to-all-start.4 = ((bf16[16,128,256]{2,1,0:T(8,128)(2,1)}), bf16[16,128,256]{2,1,0:T(8,128)(2,1)S(1)}, u32[]{:S(2)}, u32[]{:S(2)}) async-start(bf16[16,128,256]{2,1,0:T(8,128)(2,1)} %broadcast_select_fusion), calls=%async_computation.4 | async-start | bytes 2097152 | tf_op jit(solution)/shard_map/all_to_all | solution.py:140
  131.7 27.8 %all-to-all-done.4 = bf16[16,128,256]{2,1,0:T(8,128)(2,1)S(1)} async-done(((bf16[16,128,256]{2,1,0:T(8,128)(2,1)}), bf16[16,128,256]{2,1,0:T(8,128)(2,1)S(1)}, u32[]{:S(2)}, u32[]{:S(2)}) %all-to-all-start.4) | async-done | bytes 1048608 | tf_op jit(solution)/shard_map/all_to_all | solution.py:140
  160.5 0.6 broadcast_in_dim.166
  161.1 4.2 %all-to-all-start.5 = ((f32[8,8,128]{2,1,0:T(8,128)}), f32[8,8,128]{2,1,0:T(8,128)S(1)}, u32[]{:S(2)}, u32[]{:S(2)}) async-start(f32[8,8,128]{2,1,0:T(8,128)} %broadcast_in_dim.166), calls=%async_computation.5 | async-start | bytes 65536 | tf_op jit(solution)/shard_map/all_to_all | solution.py:150
  165.4 2.9 %add_convert_fusion = bf16[8,4,64,256]{3,2,1,0:T(8,128)(2,1)} fusion(bf16[8,4,64,256]{3,2,1,0:T(8,128)(2,1)} %param.23, f32[8,4]{1,0:T(8,128)S(1)} %copy.93, bf16[8,128,4,64]{1,3,2,0:T(8,128)(2,1)S(1)} %bitcast.82, f32[8,128,4]{1,2,0:T(4,128)S(1)} %copy.95, bf16[8,128,256]{2,1,0:T(8,128)(2,1)} %gather_fusion.9, pred[8]{0:T(512)(128)(4,1)S(1)} %get-tuple-element.17), kind=kOutput, calls=%fused_computation.12 | convolution fusion | flops 137363456 | bytes 3162248 | tf_op jit(solution)/shard_map/slghp,slgn->sghpn/dot_general | solution.py:64
  168.2 2.2 %all-to-all-done.5 = f32[8,8,128]{2,1,0:T(8,128)S(1)} async-done(((f32[8,8,128]{2,1,0:T(8,128)}), f32[8,8,128]{2,1,0:T(8,128)S(1)}, u32[]{:S(2)}, u32[]{:S(2)}) %all-to-all-start.5) | async-done | bytes 32800 | tf_op jit(solution)/shard_map/all_to_all | solution.py:150
  170.5 1.2 multiply_convert_fusion.3
  (80 shorter events, 4.6 us)
Async XLA Ops:
  0.6 17.0 %copy-start = (bf16[8,128,256]{2,1,0:T(8,128)(2,1)S(1)}, bf16[8,128,256]{2,1,0:T(8,128)(2,1)}, u32[]{:S(2)}) copy-start(bf16[8,128,256]{2,1,0:T(8,128)(2,1)} %param.15) | copy-start | bytes 1572868
  4.0 18.5 %all-to-all-start.3 = ((bf16[16,4,128]{2,1,0:T(4,128)(2,1)}), bf16[16,4,128]{2,1,0:T(4,128)(2,1)S(1)}, u32[]{:S(2)}, u32[]{:S(2)}) async-start(bf16[16,4,128]{2,1,0:T(4,128)(2,1)} %select_convert_fusion), calls=%async_computation.3 | async-start | bytes 32768 | tf_op jit(solution)/shard_map/all_to_all | solution.py:125
  17.7 1.7 copy-start.2
  22.4 39.5 %copy-start.8 = (s32[128]{0:T(128)S(1)}, s32[128]{0:T(128)}, u32[]{:S(2)}) copy-start(s32[128]{0:T(128)} %param.24) | copy-start | bytes 1540
  22.4 41.1 %copy-start.1 = (s32[128]{0:T(128)S(1)}, s32[128]{0:T(128)}, u32[]{:S(2)}) copy-start(s32[128]{0:T(128)} %param.25) | copy-start | bytes 1540
  58.4 30.8 %all-to-all-start.2 = ((bf16[16,128,256]{2,1,0:T(8,128)(2,1)}), bf16[16,128,256]{2,1,0:T(8,128)(2,1)S(1)}, u32[]{:S(2)}, u32[]{:S(2)}) async-start(bf16[16,128,256]{2,1,0:T(8,128)(2,1)} %get-tuple-element.24), calls=%async_computation.2 | async-start | bytes 2097152 | tf_op jit(solution)/shard_map/all_to_all | solution.py:123
  62.0 31.6 %copy-start.9 = (f32[4]{0:T(128)S(1)}, f32[4]{0:T(128)}, u32[]{:S(2)}) copy-start(f32[4]{0:T(128)} %param.20) | copy-start | bytes 52
  89.2 31.6 %all-to-all-start.1 = ((bf16[16,128,256]{2,1,0:T(8,128)(2,1)}), bf16[16,128,256]{2,1,0:T(8,128)(2,1)}, u32[]{:S(2)}, u32[]{:S(2)}) async-start(bf16[16,128,256]{2,1,0:T(8,128)(2,1)} %get-tuple-element.25), calls=%async_computation.1 | async-start | bytes 2097152 | tf_op jit(solution)/shard_map/all_to_all | solution.py:124
  99.0 25.1 %copy-start.4 = (bf16[8,4,64,256]{3,2,1,0:T(8,128)(2,1)S(1)}, bf16[8,4,64,256]{3,2,1,0:T(8,128)(2,1)}, u32[]{:S(2)}) copy-start(bf16[8,4,64,256]{3,2,1,0:T(8,128)(2,1)} %param.23) | copy-start | bytes 3145732
  122.6 2.0 %copy-start.5 = (bf16[8,128,256]{1,2,0:T(8,128)(2,1)S(1)}, bf16[8,128,256]{1,2,0:T(8,128)(2,1)}, u32[]{:S(2)}) copy-start(bf16[8,128,256]{1,2,0:T(8,128)(2,1)} %copy.85) | copy-start | bytes 1572868
  122.6 2.0 %copy-start.10 = (f32[4]{0:T(128)S(1)}, f32[4]{0:T(128)}, u32[]{:S(2)}) copy-start(f32[4]{0:T(128)} %param.21) | copy-start | bytes 52
  127.8 32.2 %copy-start.3 = (bf16[8,128,256]{2,1,0:T(8,128)(2,1)S(1)}, bf16[8,128,256]{2,1,0:T(8,128)(2,1)}, u32[]{:S(2)}) copy-start(bf16[8,128,256]{2,1,0:T(8,128)(2,1)} %param.16) | copy-start | bytes 1572868
  127.8 37.5 %copy-start.6 = (bf16[8,128,256]{1,2,0:T(8,128)(2,1)S(1)}, bf16[8,128,256]{1,2,0:T(8,128)(2,1)}, u32[]{:S(2)}) copy-start(bf16[8,128,256]{1,2,0:T(8,128)(2,1)} %copy.85) | copy-start | bytes 1572868
  127.8 31.6 %all-to-all-start.4 = ((bf16[16,128,256]{2,1,0:T(8,128)(2,1)}), bf16[16,128,256]{2,1,0:T(8,128)(2,1)S(1)}, u32[]{:S(2)}, u32[]{:S(2)}) async-start(bf16[16,128,256]{2,1,0:T(8,128)(2,1)} %broadcast_select_fusion), calls=%async_computation.4 | async-start | bytes 2097152 | tf_op jit(solution)/shard_map/all_to_all | solution.py:140
  160.0 10.5 %copy-start.7 = (f32[256]{0:T(256)S(1)}, f32[256]{0:T(256)}, u32[]{:S(2)}) copy-start(f32[256]{0:T(256)} %param.22) | copy-start | bytes 3076
  161.1 9.4 %all-to-all-start.5 = ((f32[8,8,128]{2,1,0:T(8,128)}), f32[8,8,128]{2,1,0:T(8,128)S(1)}, u32[]{:S(2)}, u32[]{:S(2)}) async-start(f32[8,8,128]{2,1,0:T(8,128)} %broadcast_in_dim.166), calls=%async_computation.5 | async-start | bytes 65536 | tf_op jit(solution)/shard_map/all_to_all | solution.py:150
